TPU v7x, 32 devices: a whole 2x2x4 slice. The times are simulated.
32 devices in a mesh: brick: 8 (over z, y), stack: 4 (over x, core).
Axes of the slice: x: 2, y: 2, z: 4, core: 2. Of those that a mesh axis runs over, the one named last changes fastest.
Arguments:
- estimate: float32 [64, 256, 128], P('stack', 'brick'), may hold values from 0.5 to 2
- view_data: float32 [6, 64, 256, 128], P(None, 'stack', 'brick'), may hold values from 0.25 to 4
- psf_taps: float32 [6, 3, 31], replicated, may hold values from 0.05 to 1
- offsets: int32 [6], replicated, may hold values from 0 to 7, as said below
- coverage: int32 [6, 8], P(None, 'brick'), may hold values from 0 to 1, as said below
Outputs:
- updated: float32 [64, 256, 128], P('stack', 'brick')
Inputs may be any that keep to these rules, and one draw needn't show every extreme that they name: Tile j of view v images brick (j + offsets[v]) mod 8. `coverage`: every brick is covered by at least one view.
All inputs are finite; a program needn't handle non-finite values.
Results may differ from a plain program's by a relative error of at most 0.0001.
Values sent between devices are 32-bit elements; how exact they have to be, the bound alone decides.
A program may use at most 128 MiB of HBM per device.

v0:
```python
import functools

import jax
import jax.numpy as jnp
from jax import lax
from jax.experimental import pallas as pl
from jax.experimental.pallas import tpu as pltpu
from jax.sharding import PartitionSpec as P

VIEWS = 6
TAPS = 31
HALF = 15
WIDTH = 128
ROWS = 32
DEPTH = 16
PAD = 16
EROWS = ROWS + 2 * PAD
EDEPTH = DEPTH + 2 * PAD
F32 = jnp.float32
BF16 = jnp.bfloat16


def split(x):
    hi = x.astype(BF16)
    lo = (x - hi.astype(F32)).astype(BF16)
    return hi, lo


def iota(shape, dim):
    return lax.broadcasted_iota(jnp.int32, shape, dim)


def spread_taps(distance, taps_ref, view, dim):
    total = jnp.float32(0.0)
    matrix = jnp.zeros(distance.shape, F32)
    for tap in range(TAPS):
        value = taps_ref[view, dim, tap]
        total = total + value
        matrix = jnp.where(distance == tap, value, matrix)
    return matrix / total


def hi_hi_lo(matrix, part):
    hi, lo = split(matrix)
    return jnp.where(part < 2, hi.astype(F32), lo.astype(F32)).astype(BF16)


def build_forward(taps_ref, wz_ref, wy_ref, wx_ref):
    def one(view, carry):
        col = iota((DEPTH, 3 * EDEPTH), 1)
        dist = col % EDEPTH - iota((DEPTH, 3 * EDEPTH), 0) - 1
        wz_ref[pl.ds(pl.multiple_of(view * DEPTH, DEPTH), DEPTH), :] = hi_hi_lo(
            spread_taps(dist, taps_ref, view, 0), col // EDEPTH
        )
        col = iota((ROWS, 3 * EROWS), 1)
        dist = col % EROWS - iota((ROWS, 3 * EROWS), 0) - 1
        wy_ref[view] = hi_hi_lo(spread_taps(dist, taps_ref, view, 1), col // EROWS)
        dist = iota((WIDTH, WIDTH), 0) - iota((WIDTH, WIDTH), 1) + HALF
        hi, lo = split(spread_taps(dist, taps_ref, view, 2))
        wx_ref[view, 0:WIDTH] = hi
        wx_ref[view, WIDTH : 2 * WIDTH] = hi
        wx_ref[view, 2 * WIDTH : 3 * WIDTH] = lo
        return carry

    lax.fori_loop(0, VIEWS, one, 0)


def build_backward(taps_ref, wz_ref, wy_ref, wx_ref, wide_ref):
    wide_ref[...] = jnp.zeros_like(wide_ref)

    def one(view, carry):
        col = iota(wide_ref.shape, 1)
        inner = col % (VIEWS * DEPTH) - view * DEPTH
        dist = iota(wide_ref.shape, 0) - inner - 1
        dist = jnp.where((inner >= 0) & (inner < DEPTH), dist, -1)
        wide_ref[...] += spread_taps(dist, taps_ref, view, 0)
        col = iota((EROWS, 3 * ROWS), 1)
        dist = iota((EROWS, 3 * ROWS), 0) - col % ROWS - 1
        wy_ref[view] = hi_hi_lo(spread_taps(dist, taps_ref, view, 1), col // ROWS)
        dist = iota((WIDTH, WIDTH), 1) - iota((WIDTH, WIDTH), 0) + HALF
        hi, lo = split(spread_taps(dist, taps_ref, view, 2))
        wx_ref[view, 0:WIDTH] = hi
        wx_ref[view, WIDTH : 2 * WIDTH] = hi
        wx_ref[view, 2 * WIDTH : 3 * WIDTH] = lo
        return carry

    lax.fori_loop(0, VIEWS, one, 0)
    wz_ref[...] = hi_hi_lo(wide_ref[...], iota(wide_ref.shape, 1) // (VIEWS * DEPTH))


def stacked(x, axis):
    hi, lo = split(x)
    return jnp.concatenate([hi, lo, hi], axis=axis)


def dot(a, b):
    return jnp.dot(a, b, preferred_element_type=F32)


def axial_forward(ext_ref, wz_ref, axial_ref):
    def one(step, carry):
        for inner in range(2):
            y = step * 4 + inner * 2
            field = jnp.concatenate(
                [ext_ref[pl.ds(y + k, EDEPTH, stride=EROWS), :] for k in range(2)], axis=1
            )
            out = dot(wz_ref[...], stacked(field, 0))
            for k in range(2):
                axial_ref[pl.ds(y + k, VIEWS * DEPTH, stride=EROWS), :] = out[
                    :, k * WIDTH : (k + 1) * WIDTH
                ]
        return carry

    lax.fori_loop(0, EROWS // 4, one, 0)


def lateral_forward(view, axial_ref, wy_ref, side_ref):
    for z in range(0, DEPTH, 2):
        base = (view * DEPTH + z) * EROWS
        field = jnp.concatenate(
            [
                axial_ref[pl.ds(pl.multiple_of(base + k * EROWS, EROWS), EROWS), :]
                for k in range(2)
            ],
            axis=1,
        )
        out = dot(wy_ref[view], stacked(field, 0))
        for k in range(2):
            side_ref[(z + k) * ROWS : (z + k + 1) * ROWS, :] = out[
                :, k * WIDTH : (k + 1) * WIDTH
            ]


def lateral_backward(view, side_ref, wy_ref, back_ref):
    for z in range(0, DEPTH, 2):
        field = jnp.concatenate(
            [side_ref[(z + k) * ROWS : (z + k + 1) * ROWS, :] for k in range(2)], axis=1
        )
        out = dot(wy_ref[view], stacked(field, 0))
        base = (view * DEPTH + z) * EROWS
        for k in range(2):
            back_ref[pl.ds(pl.multiple_of(base + k * EROWS, EROWS), EROWS), :] = out[
                :, k * WIDTH : (k + 1) * WIDTH
            ]


def axial_backward(back_ref, wz_ref, out_ref):
    def one(step, carry):
        for inner in range(2):
            y = step * 4 + inner * 2
            field = jnp.concatenate(
                [
                    back_ref[pl.ds(y + k, VIEWS * DEPTH, stride=EROWS), :]
                    for k in range(2)
                ],
                axis=1,
            )
            out = dot(wz_ref[...], stacked(field, 0))
            for k in range(2):
                out_ref[pl.ds(y + k, EDEPTH, stride=EROWS), :] = out[
                    :, k * WIDTH : (k + 1) * WIDTH
                ]
        return carry

    lax.fori_loop(0, EROWS // 4, one, 0)


CHUNK = 2
CHUNKS = VIEWS // CHUNK
CELLS = DEPTH * ROWS
SLAB = DEPTH * EROWS
EDGE = HALF * EROWS
ANY = pl.BlockSpec(memory_space=pl.ANY)
VMEM = pl.BlockSpec(memory_space=pltpu.VMEM)
SMEM = pl.BlockSpec(memory_space=pltpu.SMEM)


def kernel(
    bricks, stacks, taps_ref, offsets_ref, cover_ref, est_hbm, est_ref, view_ref, out_ref,
    mid0, mid1, mid2, stage, owned,
    halo, ext, wz, wy, wx, axial, side, blur,
    bz, by, bx, wide, back, spill, from_stack, to_brick, from_brick,
    send1, recv1, local1, send2, recv2, hsend, hrecv, ssend, srecv, tsend, trecv, usend, urecv,
):
    mids = (mid0, mid1, mid2)
    me = lax.axis_index("brick")
    level = lax.axis_index("stack")
    part = CELLS // bricks

    def to(axis, index, source, target, send_sem, recv_sem):
        return pltpu.make_async_remote_copy(
            src_ref=source,
            dst_ref=target,
            send_sem=send_sem,
            recv_sem=recv_sem,
            device_id={axis: index},
            device_id_type=pl.DeviceIdType.MESH,
        )

    def peer(step):
        return lax.rem(me + step, bricks)

    def rows(index):
        return pl.ds(pl.multiple_of(index * part, part), part)

    sides = (
        ("brick", me > 0, me - 1, 0),
        ("brick", me < bricks - 1, me + 1, 1),
    )
    floors = (
        ("stack", level > 0, level - 1, 0),
        ("stack", level < stacks - 1, level + 1, 1),
    )

    barrier = pltpu.get_barrier_semaphore()

    def greet(step, carry):
        pl.semaphore_signal(
            barrier, inc=1, device_id={"brick": peer(step)}, device_id_type=pl.DeviceIdType.MESH
        )
        return carry

    lax.fori_loop(1, bricks, greet, 0)
    for axis, there, index, _ in floors:
        @pl.when(there)
        def _():
            pl.semaphore_signal(
                barrier, inc=1, device_id={axis: index}, device_id_type=pl.DeviceIdType.MESH
            )
    pl.semaphore_wait(
        barrier,
        bricks - 1 + jnp.minimum(level, 1) + jnp.minimum(stacks - 1 - level, 1),
    )

    def halo_copy(index, up):
        source = est_hbm.at[:, pl.ds(ROWS - PAD if up else 0, PAD), :]
        return to("brick", index, source, halo.at[1 - up], hsend.at[up], hrecv.at[1 - up])

    for _, there, index, up in sides:
        @pl.when(there)
        def _():
            halo_copy(index, up).start()

    def first(step, c):
        to_index = peer(step)
        return to(
            "brick",
            to_index,
            view_ref.at[pl.ds(c * CHUNK, CHUNK), rows(to_index), :],
            mids[c].at[me],
            send1.at[c, to_index],
            recv1.at[c, me],
        )

    def first_in(step, c):
        source = peer(step)
        return to(
            "brick", source, mids[c].at[source], mids[c].at[source],
            send1.at[c, source], recv1.at[c, source],
        )

    def own(c):
        return pltpu.make_async_copy(
            view_ref.at[pl.ds(c * CHUNK, CHUNK), rows(me), :], mids[c].at[me], local1.at[c]
        )

    def second(step, c):
        to_index = peer(step)
        return to(
            "brick",
            to_index,
            stage.at[to_index, pl.ds(c * CHUNK, CHUNK)],
            owned.at[pl.ds(c * CHUNK, CHUNK), rows(me), :],
            send2.at[c, to_index],
            recv2.at[c, me],
        )

    def second_in(step, c):
        source = peer(step)
        target = owned.at[pl.ds(c * CHUNK, CHUNK), rows(source), :]
        return to("brick", source, target, target, send2.at[c, source], recv2.at[c, source])

    def each(make, act, c):
        def body(step, carry):
            act(make(step, c))
            return carry

        lax.fori_loop(1, bricks, body, 0)

    for c in range(CHUNKS):
        own(c).start()
        each(first, lambda copy: copy.start(), c)

    build_forward(taps_ref, wz, wy, wx)

    for z in (0, EDEPTH - 1):
        ext[z * EROWS : (z + 1) * EROWS, :] = jnp.zeros((EROWS, WIDTH), F32)
    for _, there, _, up in floors:
        @pl.when(jnp.logical_not(there))
        def _():
            start = (PAD + DEPTH) * EROWS if up else EROWS
            ext[start : start + EDGE, :] = jnp.zeros((EDGE, WIDTH), F32)
    for _, there, index, up in sides:
        @pl.when(there)
        def _():
            to(
                "brick", index, halo.at[up], halo.at[up], hsend.at[up], hrecv.at[up]
            ).wait_recv()

        @pl.when(jnp.logical_not(there))
        def _():
            halo[up] = jnp.zeros((DEPTH, PAD, WIDTH), F32)
    for z in range(DEPTH):
        base = (PAD + z) * EROWS
        ext[base : base + PAD, :] = halo[0, z]
        ext[base + PAD : base + PAD + ROWS, :] = est_ref[z]
        ext[base + PAD + ROWS : base + EROWS, :] = halo[1, z]

    def slab_copy(index, up):
        start = (PAD + 1 if up else PAD) * EROWS
        target = EROWS if up else (PAD + DEPTH) * EROWS
        return to(
            "stack", index, ext.at[pl.ds(start, EDGE), :], ext.at[pl.ds(target, EDGE), :],
            ssend.at[up], srecv.at[1 - up],
        )

    for _, there, index, up in floors:
        @pl.when(there)
        def _():
            slab_copy(index, up).start()
    build_backward(taps_ref, bz, by, bx, wide)
    for _, there, index, up in floors:
        @pl.when(there)
        def _():
            start = (PAD + DEPTH) * EROWS if up else EROWS
            target = ext.at[pl.ds(start, EDGE), :]
            to("stack", index, target, target, ssend.at[up], srecv.at[up]).wait_recv()
    axial_forward(ext, wz, axial)

    for c in range(CHUNKS):
        own(c).wait()
        each(first_in, lambda copy: copy.wait_recv(), c)

        def pick(target, carry, c=c):
            for k in range(CHUNK):
                view = c * CHUNK + k
                source = lax.rem(target + bricks - offsets_ref[view], bricks)
                stage[target, view] = mids[c][source, k]
            return carry

        lax.fori_loop(0, bricks, pick, 0)
        each(second, lambda copy: copy.start(), c)
        for k in range(CHUNK):
            view = c * CHUNK + k
            owned[view, rows(me), :] = stage[me, view]

        def one(view, carry):
            lateral_forward(view, axial, wy, side)
            blur[view] = dot(stacked(side[...], 1), wx[view])
            return carry

        lax.fori_loop(c * CHUNK, (c + 1) * CHUNK, one, 0)

    for c in range(CHUNKS):
        each(second_in, lambda copy: copy.wait_recv(), c)

        def one(view, carry):
            cover = cover_ref[view, 0].astype(F32)
            ratio = cover * owned[view] / blur[view]
            side[...] = dot(stacked(ratio, 1), bx[view])
            lateral_backward(view, side, by, back)
            return carry

        lax.fori_loop(c * CHUNK, (c + 1) * CHUNK, one, 0)
    axial_backward(back, bz, spill)

    def spill_copy(index, up):
        start = (PAD + DEPTH) * EROWS if up else EROWS
        return to(
            "stack", index, spill.at[pl.ds(start, EDGE), :], from_stack.at[1 - up],
            tsend.at[up], trecv.at[1 - up],
        )

    for _, there, index, up in floors:
        @pl.when(there)
        def _():
            spill_copy(index, up).start()
    for _, there, index, up in floors:
        @pl.when(there)
        def _():
            to(
                "stack", index, from_stack.at[up], from_stack.at[up], tsend.at[up], trecv.at[up]
            ).wait_recv()
            start = (PAD + 1 if up else PAD) * EROWS
            spill[start : start + EDGE, :] += from_stack[up]
            spill_copy(index, up).wait_send()
    for z in range(DEPTH):
        base = (PAD + z) * EROWS
        to_brick[0, z] = spill[base : base + PAD, :]
        to_brick[1, z] = spill[base + PAD + ROWS : base + EROWS, :]

    def side_copy(index, up):
        return to(
            "brick", index, to_brick.at[up], from_brick.at[1 - up], usend.at[up], urecv.at[1 - up]
        )

    for _, there, index, up in sides:
        @pl.when(there)
        def _():
            side_copy(index, up).start()
    count = jnp.float32(0.0)
    for view in range(VIEWS):
        count = count + cover_ref[view, 0].astype(F32)

    for c in range(CHUNKS):
        each(first, lambda copy: copy.wait_send(), c)
        each(second, lambda copy: copy.wait_send(), c)
    for _, there, index, up in sides:
        @pl.when(there)
        def _():
            halo_copy(index, up).wait_send()
    for _, there, index, up in floors:
        @pl.when(there)
        def _():
            slab_copy(index, up).wait_send()
    for _, there, index, up in sides:
        @pl.when(there)
        def _():
            to(
                "brick", index, from_brick.at[up], from_brick.at[up], usend.at[up], urecv.at[up]
            ).wait_recv()
            side_copy(index, up).wait_send()

        @pl.when(jnp.logical_not(there))
        def _():
            from_brick[up] = jnp.zeros((DEPTH, PAD, WIDTH), F32)
    for z in range(DEPTH):
        base = (PAD + z) * EROWS + PAD
        half = ROWS - PAD
        low = spill[base : base + half, :] + from_brick[0, z]
        high = spill[base + half : base + ROWS, :] + from_brick[1, z]
        out_ref[z, 0:half, :] = est_ref[z, 0:half, :] * low / count
        out_ref[z, half:ROWS, :] = est_ref[z, half:ROWS, :] * high / count


def shards(estimate, view_data, psf_taps, offsets, coverage):
    bricks = lax.axis_size("brick")
    stacks = lax.axis_size("stack")
    part = CELLS // bricks
    vmem = lambda *shape: pltpu.VMEM(shape, F32)
    half = lambda *shape: pltpu.VMEM(shape, BF16)
    sems = lambda *shape: pltpu.SemaphoreType.DMA(shape)
    scratch = [vmem(bricks, CHUNK, part, WIDTH)] * CHUNKS
    scratch += [
        vmem(bricks, VIEWS, part, WIDTH),
        vmem(VIEWS, CELLS, WIDTH),
        vmem(2, DEPTH, PAD, WIDTH),
        vmem(EDEPTH * EROWS, WIDTH),
        half(VIEWS * DEPTH, 3 * EDEPTH),
        half(VIEWS, ROWS, 3 * EROWS),
        half(VIEWS, 3 * WIDTH, WIDTH),
        vmem(VIEWS * SLAB, WIDTH),
        vmem(CELLS, WIDTH),
        vmem(VIEWS, CELLS, WIDTH),
        half(EDEPTH, 3 * VIEWS * DEPTH),
        half(VIEWS, EROWS, 3 * ROWS),
        half(VIEWS, 3 * WIDTH, WIDTH),
        vmem(EDEPTH, 3 * VIEWS * DEPTH),
        vmem(VIEWS * SLAB, WIDTH),
        vmem(EDEPTH * EROWS, WIDTH),
        vmem(2, EDGE, WIDTH),
        vmem(2, DEPTH, PAD, WIDTH),
        vmem(2, DEPTH, PAD, WIDTH),
        sems(CHUNKS, bricks),
        sems(CHUNKS, bricks),
        sems(CHUNKS),
        sems(CHUNKS, bricks),
        sems(CHUNKS, bricks),
    ]
    scratch += [sems(2)] * 8
    return pl.pallas_call(
        functools.partial(kernel, bricks, stacks),
        out_shape=jax.ShapeDtypeStruct(estimate.shape, F32),
        in_specs=[SMEM, SMEM, SMEM, ANY, VMEM, ANY],
        out_specs=VMEM,
        scratch_shapes=scratch,
        compiler_params=pltpu.CompilerParams(
            collective_id=0, has_side_effects=True, vmem_limit_bytes=48 * 1024 * 1024
        ),
    )(
        psf_taps, offsets, coverage, estimate, estimate,
        view_data.reshape(VIEWS, CELLS, WIDTH),
    )


def solution(mesh):
    placed = (
        P("stack", "brick", None),
        P(None, "stack", "brick", None),
        P(),
        P(),
        P(None, "brick"),
    )
    return jax.shard_map(
        shards, mesh=mesh, in_specs=placed, out_specs=P("stack", "brick", None), check_vma=False
    )
```

profile of v0, /device:TPU:9, one launch (start us, length us, event | category | flops | bytes accessed | tf_op | source)
XLA Modules:
  0.0 100.5 jit_solution(17502394788275310879)
XLA Ops:
  0.0 0.7 copy.6.cover_ref
  0.7 0.0 copy-start
  0.7 1.4 %copy-done = f32[6,16,32,128]{3,2,1,0:T(8,128)S(1)} copy-done((f32[6,16,32,128]{3,2,1,0:T(8,128)S(1)}, f32[6,16,32,128]{3,2,1,0:T(8,128)}, u32[]{:S(2)}) %copy-start) | copy-done | bytes 1572888
  2.1 0.0 copy-start.1
  2.2 0.9 copy-done.1
  3.1 0.0 copy-start.2
  3.1 0.7 copy-done.2
  3.8 0.0 copy-start.3
  3.8 0.7 copy-done.3
  4.5 95.3 %shard_map.55 = f32[16,32,128]{2,1,0:T(8,128)S(1)} custom-call(f32[6,3,31]{2,1,0:T(4,128)S(1)} %copy-done.2, s32[6]{0:T(128)S(1)} %copy-done.3, s32[6,1]{1,0:T(8,128)S(1)} %copy.6.cover_ref, f32[16,32,128]{2,1,0:T(8,128)S(1)} %copy-done.1, f32[16,32,128]{2,1,0:T(8,128)S(1)} %copy-done.1, f32[6,512,128]{2,1,0:T(8,128)S(1)} %bitcast.1), custom_call_target="tpu_custom_call" | custom-call | tf_op jit(solution)/shard_map/pallas_call | solution.py:481
  99.8 0.7 copy.8
Async XLA Ops:
  0.7 1.4 %copy-start = (f32[6,16,32,128]{3,2,1,0:T(8,128)S(1)}, f32[6,16,32,128]{3,2,1,0:T(8,128)}, u32[]{:S(2)}) copy-start(f32[6,16,32,128]{3,2,1,0:T(8,128)} %param.6) | copy-start | bytes 4718596
  2.1 0.9 copy-start.1
  3.1 0.7 copy-start.2
  3.8 0.7 copy-start.3
where the time goes:
time: 101 us
  Pallas kernels  95.3 us (94%)
  local copies, waits for them, and re-layouts  5.16 us (5%)
    pallas_call x1, Pallas kernels, shards(): pl.pallas_call(functools.partial(kernel, bricks, stacks), out_shape=jax.S...  95.3 us
    unnamed x10, local copies, waits for them, and re-layouts  5.16 us

commit v1 on v0

--- a/solution.py
+++ b/solution.py
@@ -69,11 +69,11 @@
     wide_ref[...] = jnp.zeros_like(wide_ref)
 
     def one(view, carry):
-        col = iota(wide_ref.shape, 1)
-        inner = col % (VIEWS * DEPTH) - view * DEPTH
-        dist = iota(wide_ref.shape, 0) - inner - 1
+        shape = wide_ref.shape[1:]
+        inner = iota(shape, 1) % (CHUNK * DEPTH) - view % CHUNK * DEPTH
+        dist = iota(shape, 0) - inner - 1
         dist = jnp.where((inner >= 0) & (inner < DEPTH), dist, -1)
-        wide_ref[...] += spread_taps(dist, taps_ref, view, 0)
+        wide_ref[view // CHUNK] += spread_taps(dist, taps_ref, view, 0)
         col = iota((EROWS, 3 * ROWS), 1)
         dist = iota((EROWS, 3 * ROWS), 0) - col % ROWS - 1
         wy_ref[view] = hi_hi_lo(spread_taps(dist, taps_ref, view, 1), col // ROWS)
@@ -85,7 +85,7 @@
         return carry
 
     lax.fori_loop(0, VIEWS, one, 0)
-    wz_ref[...] = hi_hi_lo(wide_ref[...], iota(wide_ref.shape, 1) // (VIEWS * DEPTH))
+    wz_ref[...] = hi_hi_lo(wide_ref[...], iota(wide_ref.shape, 2) // (CHUNK * DEPTH))
 
 
 def stacked(x, axis):
@@ -144,25 +144,28 @@
             ]
 
 
-def axial_backward(back_ref, wz_ref, out_ref):
+def axial_backward(c, edges, back_ref, wz_ref, out_ref):
+    half = ROWS // 2
+
     def one(step, carry):
         for inner in range(2):
-            y = step * 4 + inner * 2
+            spot = step * 4 + inner * 2
+            y = spot + (jnp.where(step >= half // 4, ROWS, 0) if edges else PAD)
             field = jnp.concatenate(
                 [
-                    back_ref[pl.ds(y + k, VIEWS * DEPTH, stride=EROWS), :]
+                    back_ref[pl.ds(c * CHUNK * SLAB + y + k, CHUNK * DEPTH, stride=EROWS), :]
                     for k in range(2)
                 ],
                 axis=1,
             )
-            out = dot(wz_ref[...], stacked(field, 0))
+            out = dot(wz_ref[c], stacked(field, 0))
             for k in range(2):
-                out_ref[pl.ds(y + k, EDEPTH, stride=EROWS), :] = out[
-                    :, k * WIDTH : (k + 1) * WIDTH
-                ]
+                place = pl.ds(spot + k, EDEPTH, stride=ROWS)
+                part = out[:, k * WIDTH : (k + 1) * WIDTH]
+                out_ref[place, :] = part if c == 0 else out_ref[place, :] + part
         return carry
 
-    lax.fori_loop(0, EROWS // 4, one, 0)
+    lax.fori_loop(0, ROWS // 4, one, 0)
 
 
 CHUNK = 2
@@ -170,17 +173,18 @@
 CELLS = DEPTH * ROWS
 SLAB = DEPTH * EROWS
 EDGE = HALF * EROWS
+BAND = HALF * ROWS
 ANY = pl.BlockSpec(memory_space=pl.ANY)
 VMEM = pl.BlockSpec(memory_space=pltpu.VMEM)
 SMEM = pl.BlockSpec(memory_space=pltpu.SMEM)
 
 
 def kernel(
-    bricks, stacks, taps_ref, offsets_ref, cover_ref, est_hbm, est_ref, view_ref, out_ref,
+    bricks, stacks, taps_ref, flags_ref, est_hbm, view_ref, out_ref, est_ref,
     mid0, mid1, mid2, stage, owned,
     halo, ext, wz, wy, wx, axial, side, blur,
-    bz, by, bx, wide, back, spill, from_stack, to_brick, from_brick,
-    send1, recv1, local1, send2, recv2, hsend, hrecv, ssend, srecv, tsend, trecv, usend, urecv,
+    bz, by, bx, wide, back, spill_edges, spill_middle, from_edges, from_middle, to_brick, from_brick,
+    send1, recv1, local1, send2, recv2, hsend, hrecv, ssend, srecv, tsend, trecv, usend, urecv, msend, mrecv, esem,
 ):
     mids = (mid0, mid1, mid2)
     me = lax.axis_index("brick")
@@ -198,7 +202,8 @@
         )
 
     def peer(step):
-        return lax.rem(me + step, bricks)
+        turn = lax.rem(step - 1 + lax.rem(level, 2) * (bricks // 2 - 1), bricks - 1)
+        return lax.rem(me + 1 + turn, bricks)
 
     def rows(index):
         return pl.ds(pl.multiple_of(index * part, part), part)
@@ -212,6 +217,8 @@
         ("stack", level < stacks - 1, level + 1, 1),
     )
 
+    load = pltpu.make_async_copy(est_hbm, est_ref, esem.at[0])
+    load.start()
     barrier = pltpu.get_barrier_semaphore()
 
     def greet(step, carry):
@@ -310,6 +317,7 @@
         @pl.when(jnp.logical_not(there))
         def _():
             halo[up] = jnp.zeros((DEPTH, PAD, WIDTH), F32)
+    load.wait()
     for z in range(DEPTH):
         base = (PAD + z) * EROWS
         ext[base : base + PAD, :] = halo[0, z]
@@ -344,7 +352,7 @@
         def pick(target, carry, c=c):
             for k in range(CHUNK):
                 view = c * CHUNK + k
-                source = lax.rem(target + bricks - offsets_ref[view], bricks)
+                source = lax.rem(target + bricks - flags_ref[view], bricks)
                 stage[target, view] = mids[c][source, k]
             return carry
 
@@ -365,39 +373,50 @@
         each(second_in, lambda copy: copy.wait_recv(), c)
 
         def one(view, carry):
-            cover = cover_ref[view, 0].astype(F32)
+            cover = flags_ref[VIEWS + view].astype(F32)
             ratio = cover * owned[view] / blur[view]
             side[...] = dot(stacked(ratio, 1), bx[view])
             lateral_backward(view, side, by, back)
             return carry
 
         lax.fori_loop(c * CHUNK, (c + 1) * CHUNK, one, 0)
-    axial_backward(back, bz, spill)
-
-    def spill_copy(index, up):
-        start = (PAD + DEPTH) * EROWS if up else EROWS
+        if c < CHUNKS - 1:
+            axial_backward(c, True, back, bz, spill_edges)
+            axial_backward(c, False, back, bz, spill_middle)
+
+    def spill_copy(index, up, source, target, send_sem, recv_sem):
+        start = (PAD + DEPTH) * ROWS if up else ROWS
         return to(
-            "stack", index, spill.at[pl.ds(start, EDGE), :], from_stack.at[1 - up],
-            tsend.at[up], trecv.at[1 - up],
-        )
-
-    for _, there, index, up in floors:
-        @pl.when(there)
-        def _():
-            spill_copy(index, up).start()
-    for _, there, index, up in floors:
-        @pl.when(there)
-        def _():
-            to(
-                "stack", index, from_stack.at[up], from_stack.at[up], tsend.at[up], trecv.at[up]
-            ).wait_recv()
-            start = (PAD + 1 if up else PAD) * EROWS
-            spill[start : start + EDGE, :] += from_stack[up]
-            spill_copy(index, up).wait_send()
+            "stack", index, source.at[pl.ds(start, BAND), :], target.at[1 - up],
+            send_sem.at[up], recv_sem.at[1 - up],
+        )
+
+    spills = (
+        (True, spill_edges, from_edges, tsend, trecv),
+        (False, spill_middle, from_middle, msend, mrecv),
+    )
+    for edges, source, target, send_sem, recv_sem in spills:
+        axial_backward(CHUNKS - 1, edges, back, bz, source)
+        for _, there, index, up in floors:
+            @pl.when(there)
+            def _():
+                spill_copy(index, up, source, target, send_sem, recv_sem).start()
+
+    def take(source, target, send_sem, recv_sem):
+        for _, there, index, up in floors:
+            @pl.when(there)
+            def _():
+                to(
+                    "stack", index, target.at[up], target.at[up], send_sem.at[up], recv_sem.at[up]
+                ).wait_recv()
+                start = (PAD + 1 if up else PAD) * ROWS
+                source[start : start + BAND, :] += target[up]
+
+    take(*spills[0][1:])
     for z in range(DEPTH):
-        base = (PAD + z) * EROWS
-        to_brick[0, z] = spill[base : base + PAD, :]
-        to_brick[1, z] = spill[base + PAD + ROWS : base + EROWS, :]
+        base = (PAD + z) * ROWS
+        to_brick[0, z] = spill_edges[base : base + PAD, :]
+        to_brick[1, z] = spill_edges[base + ROWS - PAD : base + ROWS, :]
 
     def side_copy(index, up):
         return to(
@@ -410,7 +429,7 @@
             side_copy(index, up).start()
     count = jnp.float32(0.0)
     for view in range(VIEWS):
-        count = count + cover_ref[view, 0].astype(F32)
+        count = count + flags_ref[VIEWS + view].astype(F32)
 
     for c in range(CHUNKS):
         each(first, lambda copy: copy.wait_send(), c)
@@ -423,6 +442,12 @@
         @pl.when(there)
         def _():
             slab_copy(index, up).wait_send()
+    take(*spills[1][1:])
+    for _, there, index, up in floors:
+        @pl.when(there)
+        def _():
+            for _, source, target, send_sem, recv_sem in spills:
+                spill_copy(index, up, source, target, send_sem, recv_sem).wait_send()
     for _, there, index, up in sides:
         @pl.when(there)
         def _():
@@ -435,10 +460,10 @@
         def _():
             from_brick[up] = jnp.zeros((DEPTH, PAD, WIDTH), F32)
     for z in range(DEPTH):
-        base = (PAD + z) * EROWS + PAD
+        base = (PAD + z) * ROWS
         half = ROWS - PAD
-        low = spill[base : base + half, :] + from_brick[0, z]
-        high = spill[base + half : base + ROWS, :] + from_brick[1, z]
+        low = spill_middle[base : base + half, :] + from_brick[0, z]
+        high = spill_middle[base + half : base + ROWS, :] + from_brick[1, z]
         out_ref[z, 0:half, :] = est_ref[z, 0:half, :] * low / count
         out_ref[z, half:ROWS, :] = est_ref[z, half:ROWS, :] * high / count
 
@@ -450,7 +475,7 @@
     vmem = lambda *shape: pltpu.VMEM(shape, F32)
     half = lambda *shape: pltpu.VMEM(shape, BF16)
     sems = lambda *shape: pltpu.SemaphoreType.DMA(shape)
-    scratch = [vmem(bricks, CHUNK, part, WIDTH)] * CHUNKS
+    scratch = [vmem(*estimate.shape)] + [vmem(bricks, CHUNK, part, WIDTH)] * CHUNKS
     scratch += [
         vmem(bricks, VIEWS, part, WIDTH),
         vmem(VIEWS, CELLS, WIDTH),
@@ -462,13 +487,15 @@
         vmem(VIEWS * SLAB, WIDTH),
         vmem(CELLS, WIDTH),
         vmem(VIEWS, CELLS, WIDTH),
-        half(EDEPTH, 3 * VIEWS * DEPTH),
+        half(CHUNKS, EDEPTH, 3 * CHUNK * DEPTH),
         half(VIEWS, EROWS, 3 * ROWS),
         half(VIEWS, 3 * WIDTH, WIDTH),
-        vmem(EDEPTH, 3 * VIEWS * DEPTH),
+        vmem(CHUNKS, EDEPTH, 3 * CHUNK * DEPTH),
         vmem(VIEWS * SLAB, WIDTH),
-        vmem(EDEPTH * EROWS, WIDTH),
-        vmem(2, EDGE, WIDTH),
+        vmem(EDEPTH * ROWS, WIDTH),
+        vmem(EDEPTH * ROWS, WIDTH),
+        vmem(2, BAND, WIDTH),
+        vmem(2, BAND, WIDTH),
         vmem(2, DEPTH, PAD, WIDTH),
         vmem(2, DEPTH, PAD, WIDTH),
         sems(CHUNKS, bricks),
@@ -477,18 +504,18 @@
         sems(CHUNKS, bricks),
         sems(CHUNKS, bricks),
     ]
-    scratch += [sems(2)] * 8
+    scratch += [sems(2)] * 10 + [sems(1)]
     return pl.pallas_call(
         functools.partial(kernel, bricks, stacks),
         out_shape=jax.ShapeDtypeStruct(estimate.shape, F32),
-        in_specs=[SMEM, SMEM, SMEM, ANY, VMEM, ANY],
+        in_specs=[SMEM, SMEM, ANY, ANY],
         out_specs=VMEM,
         scratch_shapes=scratch,
         compiler_params=pltpu.CompilerParams(
             collective_id=0, has_side_effects=True, vmem_limit_bytes=48 * 1024 * 1024
         ),
     )(
-        psf_taps, offsets, coverage, estimate, estimate,
+        psf_taps, jnp.concatenate([offsets, coverage[:, 0]]), estimate,
         view_data.reshape(VIEWS, CELLS, WIDTH),
     )
 

time: 101 us -> 94.4 us (0.935)
  Pallas kernels: 95.3 us -> 89.6 us
  local copies, waits for them, and re-layouts: 5.16 us -> 3.77 us
    pallas_call x1, Pallas kernels: 95.3 us -> 89.6 us  [shards(): pl.pallas_call(functools.partial(kernel, bricks, stacks), out_shape=jax.S...]
    unnamed x10 -> x7, local copies, waits for them, and re-layouts: 5.16 us -> 3.77 us
where the time goes in v1:
time: 94.4 us; the launch traced here: 94.1 us
  Pallas kernels  89.6 us (95%)
  local copies, waits for them, and re-layouts  3.77 us (4%)
    pallas_call x1, Pallas kernels, shards(): pl.pallas_call(functools.partial(kernel, bricks, stacks), out_shape=jax.S...  89.6 us
    unnamed x7, local copies, waits for them, and re-layouts  3.77 us

profile of v1, /device:TPU:9, one launch (start us, length us, event | category | flops | bytes accessed | tf_op | source)
XLA Modules:
  0.0 94.1 jit_solution(9257633755421560165)
XLA Ops:
  0.0 0.7 pad_add_fusion.flags_ref
  0.7 0.0 copy-start
  0.7 1.4 %copy-done = f32[6,16,32,128]{3,2,1,0:T(8,128)S(1)} copy-done((f32[6,16,32,128]{3,2,1,0:T(8,128)S(1)}, f32[6,16,32,128]{3,2,1,0:T(8,128)}, u32[]{:S(2)}) %copy-start) | copy-done | bytes 1572888
  2.2 0.0 copy-start.1
  2.2 0.9 %copy-done.1 = f32[16,32,128]{2,1,0:T(8,128)S(1)} copy-done((f32[16,32,128]{2,1,0:T(8,128)S(1)}, f32[16,32,128]{2,1,0:T(8,128)}, u32[]{:S(2)}) %copy-start.1) | copy-done | bytes 262168
  3.1 0.0 copy-start.2
  3.1 0.7 copy-done.2
  3.8 89.6 %shard_map.55 = f32[16,32,128]{2,1,0:T(8,128)S(1)} custom-call(f32[6,3,31]{2,1,0:T(4,128)S(1)} %copy-done.2, s32[12]{0:T(128)S(1)} %pad_add_fusion.flags_ref, f32[16,32,128]{2,1,0:T(8,128)S(1)} %copy-done.1, f32[6,512,128]{2,1,0:T(8,128)S(1)} %bitcast.2), custom_call_target="tpu_custom_call" | custom-call | tf_op jit(solution)/shard_map/pallas_call | solution.py:508
  93.4 0.7 copy.7
Async XLA Ops:
  0.7 1.4 %copy-start = (f32[6,16,32,128]{3,2,1,0:T(8,128)S(1)}, f32[6,16,32,128]{3,2,1,0:T(8,128)}, u32[]{:S(2)}) copy-start(f32[6,16,32,128]{3,2,1,0:T(8,128)} %param.6) | copy-start | bytes 4718596
  2.2 0.9 %copy-start.1 = (f32[16,32,128]{2,1,0:T(8,128)S(1)}, f32[16,32,128]{2,1,0:T(8,128)}, u32[]{:S(2)}) copy-start(f32[16,32,128]{2,1,0:T(8,128)} %est_hbm.1) | copy-start | bytes 786436
  3.1 0.7 copy-start.2

commit v2 on v1

--- a/solution.py
+++ b/solution.py
@@ -168,7 +168,7 @@
     lax.fori_loop(0, ROWS // 4, one, 0)
 
 
-CHUNK = 2
+CHUNK = 1
 CHUNKS = VIEWS // CHUNK
 CELLS = DEPTH * ROWS
 SLAB = DEPTH * EROWS
@@ -181,12 +181,12 @@
 
 def kernel(
     bricks, stacks, taps_ref, flags_ref, est_hbm, view_ref, out_ref, est_ref,
-    mid0, mid1, mid2, stage, owned,
+    mid0, mid1, mid2, mid3, mid4, mid5, stage, owned,
     halo, ext, wz, wy, wx, axial, side, blur,
     bz, by, bx, wide, back, spill_edges, spill_middle, from_edges, from_middle, to_brick, from_brick,
     send1, recv1, local1, send2, recv2, hsend, hrecv, ssend, srecv, tsend, trecv, usend, urecv, msend, mrecv, esem,
 ):
-    mids = (mid0, mid1, mid2)
+    mids = (mid0, mid1, mid2, mid3, mid4, mid5)
     me = lax.axis_index("brick")
     level = lax.axis_index("stack")
     part = CELLS // bricks
@@ -512,7 +512,7 @@
         out_specs=VMEM,
         scratch_shapes=scratch,
         compiler_params=pltpu.CompilerParams(
-            collective_id=0, has_side_effects=True, vmem_limit_bytes=48 * 1024 * 1024
+            collective_id=0, has_side_effects=True, vmem_limit_bytes=63 * 1024 * 1024
         ),
     )(
         psf_taps, jnp.concatenate([offsets, coverage[:, 0]]), estimate,

time: 94.4 us -> 100 us (1.059)
  Pallas kernels: 89.6 us -> 96.8 us
  local copies, waits for them, and re-layouts: 3.77 us -> 1.67 us
    pallas_call x1, Pallas kernels: 89.6 us -> 96.8 us  [shards(): pl.pallas_call(functools.partial(kernel, bricks, stacks), out_shape=jax.S...]
    unnamed x7 -> x1, local copies, waits for them, and re-layouts: 3.77 us -> 1.67 us
where the time goes in v2:
time: 100 us; the launch traced here: 99.8 us
  Pallas kernels  96.8 us (97%)
  local copies, waits for them, and re-layouts  1.67 us (2%)
  other arithmetic  1.26 us (1%)
    pallas_call x1, Pallas kernels, shards(): pl.pallas_call(functools.partial(kernel, bricks, stacks), out_shape=jax.S...  96.8 us

profile of v2, /device:TPU:9, one launch (start us, length us, event | category | flops | bytes accessed | tf_op | source)
XLA Modules:
  0.0 99.8 jit_solution(6946724518155959170)
XLA Ops:
  0.0 1.3 %pad_add_fusion.flags_ref = s32[12]{0:T(128)} fusion(s32[6]{0:T(128)} %bitcast.3, s32[6]{0:T(128)} %param.8), kind=kLoop, calls=%fused_computation | loop fusion | flops 12 | bytes 96 | tf_op jit(solution)/shard_map/concatenate | solution.py:518
  1.3 96.8 %shard_map.55 = f32[16,32,128]{2,1,0:T(8,128)} custom-call(f32[6,3,31]{2,1,0:T(4,128)} %taps_ref.1, s32[12]{0:T(128)} %pad_add_fusion.flags_ref, f32[16,32,128]{2,1,0:T(8,128)} %est_hbm.1, f32[6,512,128]{2,1,0:T(8,128)} %bitcast.2), custom_call_target="tpu_custom_call" | custom-call | tf_op jit(solution)/shard_map/pallas_call | solution.py:508
  98.1 1.7 %copy.7 = f32[16,32,128]{2,1,0:T(8,128)} copy(f32[16,32,128]{2,1,0:T(8,128)} %shard_map.55) | data formatting | bytes 524288

commit v3 on v1

--- a/solution.py
+++ b/solution.py
@@ -168,7 +168,7 @@
     lax.fori_loop(0, ROWS // 4, one, 0)
 
 
-CHUNK = 2
+CHUNK = 3
 CHUNKS = VIEWS // CHUNK
 CELLS = DEPTH * ROWS
 SLAB = DEPTH * EROWS
@@ -181,12 +181,12 @@
 
 def kernel(
     bricks, stacks, taps_ref, flags_ref, est_hbm, view_ref, out_ref, est_ref,
-    mid0, mid1, mid2, stage, owned,
+    mid0, mid1, stage, owned,
     halo, ext, wz, wy, wx, axial, side, blur,
     bz, by, bx, wide, back, spill_edges, spill_middle, from_edges, from_middle, to_brick, from_brick,
     send1, recv1, local1, send2, recv2, hsend, hrecv, ssend, srecv, tsend, trecv, usend, urecv, msend, mrecv, esem,
 ):
-    mids = (mid0, mid1, mid2)
+    mids = (mid0, mid1)
     me = lax.axis_index("brick")
     level = lax.axis_index("stack")
     part = CELLS // bricks

time: 94.4 us -> 93.9 us (level)
  no operation moved by 1% of the time
where the time goes in v3:
time: 93.9 us; the launch traced here: 93.6 us
  Pallas kernels  89.1 us (95%)
  local copies, waits for them, and re-layouts  3.77 us (4%)
    pallas_call x1, Pallas kernels, shards(): pl.pallas_call(functools.partial(kernel, bricks, stacks), out_shape=jax.S...  89.1 us
    unnamed x7, local copies, waits for them, and re-layouts  3.77 us

profile of v3, /device:TPU:9, one launch (start us, length us, event | category | flops | bytes accessed | tf_op | source)
XLA Modules:
  0.0 93.6 jit_solution(5159091420491173393)
XLA Ops:
  0.0 0.7 pad_add_fusion.flags_ref
  0.7 0.0 copy-start
  0.7 1.4 %copy-done = f32[6,16,32,128]{3,2,1,0:T(8,128)S(1)} copy-done((f32[6,16,32,128]{3,2,1,0:T(8,128)S(1)}, f32[6,16,32,128]{3,2,1,0:T(8,128)}, u32[]{:S(2)}) %copy-start) | copy-done | bytes 1572888
  2.2 0.0 copy-start.1
  2.2 0.9 %copy-done.1 = f32[16,32,128]{2,1,0:T(8,128)S(1)} copy-done((f32[16,32,128]{2,1,0:T(8,128)S(1)}, f32[16,32,128]{2,1,0:T(8,128)}, u32[]{:S(2)}) %copy-start.1) | copy-done | bytes 262168
  3.1 0.0 copy-start.2
  3.1 0.7 copy-done.2
  3.8 89.1 %shard_map.55 = f32[16,32,128]{2,1,0:T(8,128)S(1)} custom-call(f32[6,3,31]{2,1,0:T(4,128)S(1)} %copy-done.2, s32[12]{0:T(128)S(1)} %pad_add_fusion.flags_ref, f32[16,32,128]{2,1,0:T(8,128)S(1)} %copy-done.1, f32[6,512,128]{2,1,0:T(8,128)S(1)} %bitcast.2), custom_call_target="tpu_custom_call" | custom-call | tf_op jit(solution)/shard_map/pallas_call | solution.py:508
  92.9 0.7 copy.7
Async XLA Ops:
  0.7 1.4 %copy-start = (f32[6,16,32,128]{3,2,1,0:T(8,128)S(1)}, f32[6,16,32,128]{3,2,1,0:T(8,128)}, u32[]{:S(2)}) copy-start(f32[6,16,32,128]{3,2,1,0:T(8,128)} %param.6) | copy-start | bytes 4718596
  2.2 0.9 %copy-start.1 = (f32[16,32,128]{2,1,0:T(8,128)S(1)}, f32[16,32,128]{2,1,0:T(8,128)}, u32[]{:S(2)}) copy-start(f32[16,32,128]{2,1,0:T(8,128)} %est_hbm.1) | copy-start | bytes 786436
  3.1 0.7 copy-start.2
